TPU v7x, 512 devices: a whole 4x4x16 slice. The times are simulated.
512 devices in a mesh: domain: 8 (over x, core), fsdp: 64 (over y, z).
Axes of the slice: x: 4, y: 4, z: 16, core: 2. Of those that a mesh axis runs over, the one named last changes fastest.
Arguments:
- gradients: bfloat16 [8, 64, 4096, 512], P('domain', None, 'fsdp')
- row_counts: int32 [64], replicated, may hold values from 2048 to 4096, as said below
- domain_ids: int32 [8], replicated, may hold values from 0 to 7
- domain_weights: float32 [8], replicated, may hold values from 0.2 to 2
Outputs:
- updates: float32 [64, 4096, 512], P('domain', 'fsdp')
- new_weights: float32 [8], replicated
Inputs may be any that keep to these rules, and one draw needn't show every extreme that they name: `row_counts`: each matrix has 4096 or 2048 rows, and both counts occur.
All inputs are finite; a program needn't handle non-finite values.
Results may differ from a plain program's by a relative error of at most 0.0071.
Values may be sent and summed in bfloat16 or wider, within the bound.
A program may use at most 64 MiB of HBM per device.

v0:
```python
import math
import jax
import jax.numpy as jnp
from jax import lax
from jax.sharding import PartitionSpec as P

NS_ITERS = 3
OWNERS = 8
COEF_A = 3.4445
COEF_B = -4.775
COEF_C = 2.0315
MUON_SCALE = 0.2
ETA = 4.0


def partner(shard, axis, stride):
    return lax.ppermute(shard, axis, [(i, i ^ 1 << stride) for i in range(lax.axis_size(axis))])


def group_mixing(domain_ids, domain_weights, kind_count):
    weight_share = domain_weights / jnp.sum(domain_weights)
    onehot = (domain_ids[:, None] == jnp.arange(kind_count, dtype=jnp.int32)[None, :]).astype(
        jnp.float32
    )
    counts = jnp.sum(onehot, axis=0)
    per_member = weight_share / jnp.maximum(counts, 1.0)
    group_mix = jnp.sum(onehot * per_member[None, :], axis=1)
    return (weight_share, onehot, counts, group_mix)


def summed_gram(iterate):
    gram_total = lax.dot_general(
        iterate, iterate, (((0,), (0,)), ((), ())), preferred_element_type=jnp.float32
    )
    for bit_pos in range(OWNERS.bit_length() - 1):
        gram_total = gram_total + partner(gram_total, "fsdp", bit_pos)
    return gram_total


def newton_steps(iterate):
    for repeat in range(NS_ITERS):
        gram_full = lax.optimization_barrier(summed_gram(iterate).astype(jnp.bfloat16))
        square = jnp.dot(gram_full, gram_full, preferred_element_type=jnp.float32)
        poly_term = (COEF_B * gram_full.astype(jnp.float32) + COEF_C * square).astype(jnp.bfloat16)
        iterate = lax.optimization_barrier(
            (
                COEF_A * iterate.astype(jnp.float32)
                + jnp.dot(iterate, poly_term, preferred_element_type=jnp.float32)
            ).astype(jnp.bfloat16)
        )
    return iterate


def share_scores(aligned, squares, norm_slots):
    return lax.psum((aligned, squares, norm_slots), ("domain", "fsdp"))


def body(gradients, row_counts, domain_ids, domain_weights):
    groups = lax.axis_size("domain")
    shards = lax.axis_size("fsdp")
    matrices = row_counts.shape[0]
    rows_src = gradients.shape[2]
    columns = gradients.shape[3]
    per_domain = matrices // groups
    sub_rows = rows_src // OWNERS
    own_rows = shards * sub_rows
    full_rows = rows_src * shards
    domain_pos = lax.axis_index("domain")
    shard_pos = lax.axis_index("fsdp")
    matrix_index = domain_pos * per_domain + shard_pos // OWNERS
    owner_rank = shard_pos % OWNERS
    source = jnp.arange(shards, dtype=jnp.int32)[:, None]
    within = jnp.arange(sub_rows, dtype=jnp.int32)[None, :]
    owner_rows = (source * rows_src + owner_rank * sub_rows + within).reshape(own_rows)
    weight_share, onehot, counts, group_mix = group_mixing(
        domain_ids, domain_weights, domain_weights.shape[0]
    )
    sectioned = gradients.reshape(1, groups, shards, sub_rows, columns)
    received = lax.all_to_all(
        lax.all_to_all(sectioned, "domain", split_axis=1, concat_axis=0, tiled=True),
        "fsdp",
        split_axis=2,
        concat_axis=3,
        tiled=True,
    )
    received = received.reshape(groups, own_rows, columns)
    row_limit = lax.dynamic_index_in_dim(row_counts, matrix_index, 0, keepdims=False)
    row_mask = (owner_rows < row_limit)[None, :, None]
    masked = jnp.where(row_mask, received.astype(jnp.float32), jnp.zeros((), jnp.float32))
    combined = jnp.sum(group_mix[:, None, None] * masked, axis=0)
    aligned = jnp.sum(masked * combined[None], axis=(1, 2))
    squares = jnp.sum(masked * masked, axis=(1, 2))
    own_square = jnp.sum(combined * combined)
    norm_slots = jnp.where(
        jnp.arange(matrices, dtype=jnp.int32) == matrix_index,
        own_square,
        jnp.zeros((), jnp.float32),
    )
    aligned, squares, norm_slots = share_scores(aligned, squares, norm_slots)
    frob_norm = (
        jnp.sqrt(lax.dynamic_index_in_dim(norm_slots, matrix_index, 0, keepdims=False)) + 1e-07
    )
    start_rows = lax.optimization_barrier((combined / frob_norm).astype(jnp.bfloat16))
    finished = newton_steps(start_rows)
    returned = lax.all_to_all(
        finished.reshape(1, shards, sub_rows, columns),
        "fsdp",
        split_axis=1,
        concat_axis=0,
        tiled=True,
    )
    returned = returned.reshape(per_domain, rows_src, columns)
    updates = returned.astype(jnp.float32) * (MUON_SCALE * math.sqrt(full_rows))
    total_sq = jnp.sum(norm_slots)
    cosine = aligned / (jnp.sqrt(squares) * jnp.sqrt(total_sq) + 1e-06)
    score = jnp.sum(onehot * cosine[:, None], axis=0) / jnp.maximum(counts, 1.0)
    raised = weight_share * jnp.exp(ETA * score)
    return (updates, raised / jnp.sum(raised))


def solution(mesh):
    placed = (P("domain", None, "fsdp", None), P(), P(), P())
    return jax.shard_map(
        body,
        mesh=mesh,
        in_specs=placed,
        out_specs=(P("domain", "fsdp", None), P()),
        check_vma=False,
    )
```

profile of v0, /device:TPU:8, one launch (start us, length us, event | category | flops | bytes accessed | tf_op | source)
XLA Modules:
  0.0 937.1 jit_solution(9981151052940490858)
XLA Ops:
  0.6 54.6 %all_to_all.30 = bf16[1,8,64,8,512]{4,3,2,0,1:T(8,128)(2,1)S(1)} all-to-all(bf16[1,8,64,8,512]{4,3,2,0,1:T(8,128)(2,1)} %bitcast.26), channel_id=1, replica_groups=mesh['domain'=8,'fsdp'=64] {'domain'}, dimensions={1} | all-to-all | bytes 8388608 | tf_op jit(solution)/shard_map/all_to_all | solution.py:80
  55.3 2.6 copy.8
  57.9 19.1 %all-to-all-start.1 = ((bf16[8,1,64,8,512]{4,3,0,1,2:T(8,128)(2,1)}), bf16[8,1,64,8,512]{4,3,0,1,2:T(8,128)(2,1)}, u32[]{:S(2)}, u32[]{:S(2)}) async-start(bf16[8,1,64,8,512]{4,3,0,1,2:T(8,128)(2,1)} %copy.8), calls=%async_computation.1 | async-start | bytes 8388608 | tf_op jit(solution)/shard_map/all_to_all | solution.py:79
  77.0 0.6 reduce_sum.90
  77.6 0.6 dynamic_slice.8
  78.2 0.7 multiply_divide_fusion
  79.1 0.7 add_compare_fusion
  79.8 182.4 %all-to-all-done.1 = bf16[8,1,64,8,512]{4,3,0,1,2:T(8,128)(2,1)} async-done(((bf16[8,1,64,8,512]{4,3,0,1,2:T(8,128)(2,1)}), bf16[8,1,64,8,512]{4,3,0,1,2:T(8,128)(2,1)}, u32[]{:S(2)}, u32[]{:S(2)}) %all-to-all-start.1) | async-done | bytes 4194336 | tf_op jit(solution)/shard_map/all_to_all | solution.py:79
  262.2 4.3 multiply_reduce_fusion.2
  266.5 0.9 multiply_reduce_fusion.3
  267.4 0.6 compare_select_fusion
  268.0 4.3 multiply_reduce_fusion
  272.3 99.8 %all-reduce = (f32[64]{0:T(128)S(1)}, f32[8]{0:T(128)S(1)}, f32[8]{0:T(128)S(1)}) all-reduce(f32[64]{0:T(128)S(1)} %compare_select_fusion, f32[8]{0:T(128)S(1)} %get-tuple-element.3, f32[8]{0:T(128)S(1)} %get-tuple-element.2), channel_id=1, replica_groups=mesh['domain'=8,'fsdp'=64] {'domain','fsdp'}, use_global_device_ids=true, to_apply=%region_5.6 | all-reduce | flops 80 | bytes 640 | tf_op jit(solution)/shard_map/psum | solution.py:55
  372.1 0.6 dynamic_slice.9
  373.5 0.5 fusion.17
  374.0 3.8 collective-permute-start
  377.7 23.2 %collective-permute-done = f32[512,512]{1,0:T(8,128)S(1)} collective-permute-done((f32[512,512]{1,0:T(8,128)S(1)}, f32[512,512]{1,0:T(8,128)S(1)}, u32[]{:S(2)}, u32[]{:S(2)}) %collective-permute-start) | collective-permute-done | bytes 1048608 | tf_op jit(solution)/shard_map/ppermute | solution.py:17
  401.1 3.1 collective-permute-start.1
  404.1 46.4 %collective-permute-done.1 = f32[512,512]{1,0:T(8,128)S(1)} collective-permute-done((f32[512,512]{1,0:T(8,128)S(1)}, f32[512,512]{1,0:T(8,128)S(1)}, u32[]{:S(2)}, u32[]{:S(2)}) %collective-permute-start.1) | collective-permute-done | bytes 1048608 | tf_op jit(solution)/shard_map/ppermute | solution.py:17
  450.5 0.2 add.114
  450.7 5.4 collective-permute-start.2
  456.1 90.8 %collective-permute-done.2 = f32[512,512]{1,0:T(8,128)S(1)} collective-permute-done((f32[512,512]{1,0:T(8,128)S(1)}, f32[512,512]{1,0:T(8,128)S(1)}, u32[]{:S(2)}, u32[]{:S(2)}) %collective-permute-start.2) | collective-permute-done | bytes 1048608 | tf_op jit(solution)/shard_map/ppermute | solution.py:17
  546.9 0.3 add_convert_fusion.5
  547.2 0.8 fusion
  547.9 0.5 fusion.18
  548.4 1.9 collective-permute-start.3
  550.3 25.0 %collective-permute-done.3 = f32[512,512]{1,0:T(8,128)S(1)} collective-permute-done((f32[512,512]{1,0:T(8,128)S(1)}, f32[512,512]{1,0:T(8,128)S(1)}, u32[]{:S(2)}, u32[]{:S(2)}) %collective-permute-start.3) | collective-permute-done | bytes 1048608 | tf_op jit(solution)/shard_map/ppermute | solution.py:17
  575.6 1.9 collective-permute-start.4
  577.5 47.6 %collective-permute-done.4 = f32[512,512]{1,0:T(8,128)S(1)} collective-permute-done((f32[512,512]{1,0:T(8,128)S(1)}, f32[512,512]{1,0:T(8,128)S(1)}, u32[]{:S(2)}, u32[]{:S(2)}) %collective-permute-start.4) | collective-permute-done | bytes 1048608 | tf_op jit(solution)/shard_map/ppermute | solution.py:17
  625.3 3.6 collective-permute-start.5
  628.9 90.8 %collective-permute-done.5 = f32[512,512]{1,0:T(8,128)S(1)} collective-permute-done((f32[512,512]{1,0:T(8,128)S(1)}, f32[512,512]{1,0:T(8,128)S(1)}, u32[]{:S(2)}, u32[]{:S(2)}) %collective-permute-start.5) | collective-permute-done | bytes 1048608 | tf_op jit(solution)/shard_map/ppermute | solution.py:17
  719.7 0.3 add_convert_fusion.3
  720.0 0.8 fusion.1
  720.8 0.5 fusion.19
  721.3 1.9 collective-permute-start.6
  723.2 25.0 %collective-permute-done.6 = f32[512,512]{1,0:T(8,128)S(1)} collective-permute-done((f32[512,512]{1,0:T(8,128)S(1)}, f32[512,512]{1,0:T(8,128)S(1)}, u32[]{:S(2)}, u32[]{:S(2)}) %collective-permute-start.6) | collective-permute-done | bytes 1048608 | tf_op jit(solution)/shard_map/ppermute | solution.py:17
  748.4 1.9 collective-permute-start.7
  750.4 47.6 %collective-permute-done.7 = f32[512,512]{1,0:T(8,128)S(1)} collective-permute-done((f32[512,512]{1,0:T(8,128)S(1)}, f32[512,512]{1,0:T(8,128)S(1)}, u32[]{:S(2)}, u32[]{:S(2)}) %collective-permute-start.7) | collective-permute-done | bytes 1048608 | tf_op jit(solution)/shard_map/ppermute | solution.py:17
  798.1 3.6 collective-permute-start.8
  801.7 90.8 %collective-permute-done.8 = f32[512,512]{1,0:T(8,128)S(1)} collective-permute-done((f32[512,512]{1,0:T(8,128)S(1)}, f32[512,512]{1,0:T(8,128)S(1)}, u32[]{:S(2)}, u32[]{:S(2)}) %collective-permute-start.8) | collective-permute-done | bytes 1048608 | tf_op jit(solution)/shard_map/ppermute | solution.py:17
  892.5 0.3 add_convert_fusion.1
  892.7 1.6 fusion.2
  894.3 9.8 %all-to-all-start.2 = ((bf16[1,64,8,512]{3,2,0,1:T(8,128)(2,1)}), bf16[1,64,8,512]{3,2,0,1:T(8,128)(2,1)S(1)}, u32[]{:S(2)}, u32[]{:S(2)}) async-start(bf16[1,64,8,512]{3,2,0,1:T(8,128)(2,1)} %bitcast.6), calls=%async_computation.2 | async-start | bytes 1048576 | tf_op jit(solution)/shard_map/all_to_all | solution.py:105
  904.2 0.7 reduce_sum.97
  905.7 1.3 fusion.16
  907.0 1.2 broadcast_divide_fusion
  908.2 27.8 %all-to-all-done.2 = bf16[1,64,8,512]{3,2,0,1:T(8,128)(2,1)S(1)} async-done(((bf16[1,64,8,512]{3,2,0,1:T(8,128)(2,1)}), bf16[1,64,8,512]{3,2,0,1:T(8,128)(2,1)S(1)}, u32[]{:S(2)}, u32[]{:S(2)}) %all-to-all-start.2) | async-done | bytes 524320 | tf_op jit(solution)/shard_map/all_to_all | solution.py:105
  936.0 1.1 convert_multiply_fusion
  (17 shorter events, 1.5 us)
Async XLA Ops:
  57.9 19.1 %copy-start = (f32[8]{0:T(128)S(1)}, f32[8]{0:T(128)}, u32[]{:S(2)}) copy-start(f32[8]{0:T(128)} %param.7) | copy-start | bytes 100
  57.9 19.7 %copy-start.1 = (s32[64]{0:T(128)S(1)}, s32[64]{0:T(128)}, u32[]{:S(2)}) copy-start(s32[64]{0:T(128)} %param.5) | copy-start | bytes 772
  57.9 20.3 %copy-start.2 = (s32[8]{0:T(128)S(1)}, s32[8]{0:T(128)}, u32[]{:S(2)}) copy-start(s32[8]{0:T(128)} %param.6) | copy-start | bytes 100
  57.9 204.3 %all-to-all-start.1 = ((bf16[8,1,64,8,512]{4,3,0,1,2:T(8,128)(2,1)}), bf16[8,1,64,8,512]{4,3,0,1,2:T(8,128)(2,1)}, u32[]{:S(2)}, u32[]{:S(2)}) async-start(bf16[8,1,64,8,512]{4,3,0,1,2:T(8,128)(2,1)} %copy.8), calls=%async_computation.1 | async-start | bytes 8388608 | tf_op jit(solution)/shard_map/all_to_all | solution.py:79
  374.0 26.9 %collective-permute-start = (f32[512,512]{1,0:T(8,128)S(1)}, f32[512,512]{1,0:T(8,128)S(1)}, u32[]{:S(2)}, u32[]{:S(2)}) collective-permute-start(f32[512,512]{1,0:T(8,128)S(1)} %fusion.17), channel_id=1, source_target_pairs={{0,1},{1,0},{2,3},{3,2},{4,5},{5,4},{6,7},{7,6},{8,9},{9,8},{10,11... | collective-permute-start | bytes 3145736 | tf_op jit(solution)/shard_map/ppermute | solution.py:17
  401.1 49.4 %collective-permute-start.1 = (f32[512,512]{1,0:T(8,128)S(1)}, f32[512,512]{1,0:T(8,128)S(1)}, u32[]{:S(2)}, u32[]{:S(2)}) collective-permute-start(f32[512,512]{1,0:T(8,128)S(1)} %add.113), channel_id=1, source_target_pairs={{0,2},{1,3},{2,0},{3,1},{4,6},{5,7},{6,4},{7,5},{8,10},{9,11},{10,... | collective-permute-start | bytes 3145736 | tf_op jit(solution)/shard_map/ppermute | solution.py:17
  450.7 96.2 %collective-permute-start.2 = (f32[512,512]{1,0:T(8,128)S(1)}, f32[512,512]{1,0:T(8,128)S(1)}, u32[]{:S(2)}, u32[]{:S(2)}) collective-permute-start(f32[512,512]{1,0:T(8,128)S(1)} %add.114), channel_id=1, source_target_pairs={{0,4},{1,5},{2,6},{3,7},{4,0},{5,1},{6,2},{7,3},{8,12},{9,13},{10,... | collective-permute-start | bytes 3145736 | tf_op jit(solution)/shard_map/ppermute | solution.py:17
  548.4 27.0 %collective-permute-start.3 = (f32[512,512]{1,0:T(8,128)S(1)}, f32[512,512]{1,0:T(8,128)S(1)}, u32[]{:S(2)}, u32[]{:S(2)}) collective-permute-start(f32[512,512]{1,0:T(8,128)S(1)} %fusion.18), channel_id=1, source_target_pairs={{0,1},{1,0},{2,3},{3,2},{4,5},{5,4},{6,7},{7,6},{8,9},{9,8},{10,11... | collective-permute-start | bytes 3145736 | tf_op jit(solution)/shard_map/ppermute | solution.py:17
  575.6 49.5 %collective-permute-start.4 = (f32[512,512]{1,0:T(8,128)S(1)}, f32[512,512]{1,0:T(8,128)S(1)}, u32[]{:S(2)}, u32[]{:S(2)}) collective-permute-start(f32[512,512]{1,0:T(8,128)S(1)} %add.118), channel_id=1, source_target_pairs={{0,2},{1,3},{2,0},{3,1},{4,6},{5,7},{6,4},{7,5},{8,10},{9,11},{10,... | collective-permute-start | bytes 3145736 | tf_op jit(solution)/shard_map/ppermute | solution.py:17
  625.3 94.4 %collective-permute-start.5 = (f32[512,512]{1,0:T(8,128)S(1)}, f32[512,512]{1,0:T(8,128)S(1)}, u32[]{:S(2)}, u32[]{:S(2)}) collective-permute-start(f32[512,512]{1,0:T(8,128)S(1)} %add.119), channel_id=1, source_target_pairs={{0,4},{1,5},{2,6},{3,7},{4,0},{5,1},{6,2},{7,3},{8,12},{9,13},{10,... | collective-permute-start | bytes 3145736 | tf_op jit(solution)/shard_map/ppermute | solution.py:17
  721.3 27.0 %collective-permute-start.6 = (f32[512,512]{1,0:T(8,128)S(1)}, f32[512,512]{1,0:T(8,128)S(1)}, u32[]{:S(2)}, u32[]{:S(2)}) collective-permute-start(f32[512,512]{1,0:T(8,128)S(1)} %fusion.19), channel_id=1, source_target_pairs={{0,1},{1,0},{2,3},{3,2},{4,5},{5,4},{6,7},{7,6},{8,9},{9,8},{10,11... | collective-permute-start | bytes 3145736 | tf_op jit(solution)/shard_map/ppermute | solution.py:17
  748.4 49.5 %collective-permute-start.7 = (f32[512,512]{1,0:T(8,128)S(1)}, f32[512,512]{1,0:T(8,128)S(1)}, u32[]{:S(2)}, u32[]{:S(2)}) collective-permute-start(f32[512,512]{1,0:T(8,128)S(1)} %add.123), channel_id=1, source_target_pairs={{0,2},{1,3},{2,0},{3,1},{4,6},{5,7},{6,4},{7,5},{8,10},{9,11},{10,... | collective-permute-start | bytes 3145736 | tf_op jit(solution)/shard_map/ppermute | solution.py:17
  798.1 94.4 %collective-permute-start.8 = (f32[512,512]{1,0:T(8,128)S(1)}, f32[512,512]{1,0:T(8,128)S(1)}, u32[]{:S(2)}, u32[]{:S(2)}) collective-permute-start(f32[512,512]{1,0:T(8,128)S(1)} %add.124), channel_id=1, source_target_pairs={{0,4},{1,5},{2,6},{3,7},{4,0},{5,1},{6,2},{7,3},{8,12},{9,13},{10,... | collective-permute-start | bytes 3145736 | tf_op jit(solution)/shard_map/ppermute | solution.py:17
  894.3 41.7 %all-to-all-start.2 = ((bf16[1,64,8,512]{3,2,0,1:T(8,128)(2,1)}), bf16[1,64,8,512]{3,2,0,1:T(8,128)(2,1)S(1)}, u32[]{:S(2)}, u32[]{:S(2)}) async-start(bf16[1,64,8,512]{3,2,0,1:T(8,128)(2,1)} %bitcast.6), calls=%async_computation.2 | async-start | bytes 1048576 | tf_op jit(solution)/shard_map/all_to_all | solution.py:105
where the time goes:
time: 938 us; the launch traced here: 937 us
  waiting for transfers between devices  697 us (74%)
  blocking collectives  154 us (16%)
  starting transfers between devices  56 us (6%)
  other arithmetic  18.9 us (2%)
    ppermute x9, waiting for transfers between devices, partner(): lax.ppermute(shard, axis, [(i, i ^ 1 << stride) for i in range(lax.axis_s...  487 us
    all_to_all x1, waiting for transfers between devices, body(): lax.all_to_all(lax.all_to_all(sectioned, 'domain', split_axis=1, concat_a...  182 us
    psum x1, blocking collectives, share_scores(): return lax.psum((aligned, squares, norm_slots), ('domain', 'fsdp'))  99.8 us
    all_to_all x1, blocking collectives, body(): lax.all_to_all(sectioned, 'domain', split_axis=1, concat_axis=0, tiled=True)  54.6 us
    all_to_all x1, waiting for transfers between devices, body(): lax.all_to_all(finished.reshape(1, shards, sub_rows, columns), 'fsdp', sp...  27.8 us
    ppermute x9, starting transfers between devices, partner(): lax.ppermute(shard, axis, [(i, i ^ 1 << stride) for i in range(lax.axis_s...  27.1 us
    all_to_all x1, starting transfers between devices, body(): lax.all_to_all(lax.all_to_all(sectioned, 'domain', split_axis=1, concat_a...  19.1 us
  transfers between devices with their start and end apart: 11, of which 11 were waited for; matrix products, arithmetic and copies ran while one was open for 1% of the time, Pallas kernels for 0%

commit v1 on v0

--- a/solution.py
+++ b/solution.py
@@ -52,7 +52,7 @@
 
 
 def share_scores(aligned, squares, norm_slots):
-    return lax.psum((aligned, squares, norm_slots), ("domain", "fsdp"))
+    return lax.psum(lax.psum((aligned, squares, norm_slots), "domain"), "fsdp")
 
 
 def body(gradients, row_counts, domain_ids, domain_weights):

time: 938 us -> 879 us (0.937)
  waiting for transfers between devices: 697 us -> 540 us
  starting transfers between devices: 56 us -> 120 us
  blocking collectives: 154 us -> 188 us
    ppermute x9, waiting for transfers between devices: 487 us -> 340 us  [partner(): lax.ppermute(shard, axis, [(i, i ^ 1 << stride) for i in range(lax.axis_s...]
    ppermute x9, starting transfers between devices: 27.1 us -> 74.3 us  [partner(): lax.ppermute(shard, axis, [(i, i ^ 1 << stride) for i in range(lax.axis_s...]
    psum x1 -> x2, blocking collectives: 99.8 us -> 134 us  [share_scores(): return lax.psum(lax.psum((aligned, squares, norm_slots), 'domain'), 'fsdp')]
    all_to_all x1, starting transfers between devices: 9.81 us -> 27 us  [body(): lax.all_to_all(finished.reshape(1, shards, sub_rows, columns), 'fsdp', sp...]
    all_to_all x1, waiting for transfers between devices: 27.8 us -> 17.6 us  [body(): lax.all_to_all(finished.reshape(1, shards, sub_rows, columns), 'fsdp', sp...]
where the time goes in v1:
time: 879 us; the launch traced here: 878 us
  waiting for transfers between devices  540 us (61%)
  blocking collectives  188 us (21%)
  starting transfers between devices  120 us (14%)
  other arithmetic  18.9 us (2%)
    ppermute x9, waiting for transfers between devices, partner(): lax.ppermute(shard, axis, [(i, i ^ 1 << stride) for i in range(lax.axis_s...  340 us
    all_to_all x1, waiting for transfers between devices, body(): lax.all_to_all(lax.all_to_all(sectioned, 'domain', split_axis=1, concat_a...  182 us
    psum x2, blocking collectives, share_scores(): return lax.psum(lax.psum((aligned, squares, norm_slots), 'domain'), 'fsdp')  134 us
    ppermute x9, starting transfers between devices, partner(): lax.ppermute(shard, axis, [(i, i ^ 1 << stride) for i in range(lax.axis_s...  74.3 us
    all_to_all x1, blocking collectives, body(): lax.all_to_all(sectioned, 'domain', split_axis=1, concat_axis=0, tiled=True)  54.6 us
    all_to_all x1, starting transfers between devices, body(): lax.all_to_all(finished.reshape(1, shards, sub_rows, columns), 'fsdp', sp...  27 us
    all_to_all x1, starting transfers between devices, body(): lax.all_to_all(lax.all_to_all(sectioned, 'domain', split_axis=1, concat_a...  19.1 us
    all_to_all x1, waiting for transfers between devices, body(): lax.all_to_all(finished.reshape(1, shards, sub_rows, columns), 'fsdp', sp...  17.6 us
  transfers between devices with their start and end apart: 11, of which 11 were waited for; matrix products, arithmetic and copies ran while one was open for 1% of the time, Pallas kernels for 0%

profile of v1, /device:TPU:8, one launch (start us, length us, event | category | flops | bytes accessed | tf_op | source)
XLA Modules:
  0.0 878.4 jit_solution(14256214146503913212)
XLA Ops:
  0.6 54.6 %all_to_all.30 = bf16[1,8,64,8,512]{4,3,2,0,1:T(8,128)(2,1)S(1)} all-to-all(bf16[1,8,64,8,512]{4,3,2,0,1:T(8,128)(2,1)} %bitcast.26), channel_id=1, replica_groups=mesh['domain'=8,'fsdp'=64] {'domain'}, dimensions={1} | all-to-all | bytes 8388608 | tf_op jit(solution)/shard_map/all_to_all | solution.py:80
  55.3 2.6 copy.8
  57.9 19.1 %all-to-all-start.1 = ((bf16[8,1,64,8,512]{4,3,0,1,2:T(8,128)(2,1)}), bf16[8,1,64,8,512]{4,3,0,1,2:T(8,128)(2,1)}, u32[]{:S(2)}, u32[]{:S(2)}) async-start(bf16[8,1,64,8,512]{4,3,0,1,2:T(8,128)(2,1)} %copy.8), calls=%async_computation.1 | async-start | bytes 8388608 | tf_op jit(solution)/shard_map/all_to_all | solution.py:79
  77.0 0.6 reduce_sum.90
  77.6 0.6 dynamic_slice.8
  78.2 0.7 multiply_divide_fusion
  79.1 0.7 add_compare_fusion
  79.8 182.4 %all-to-all-done.1 = bf16[8,1,64,8,512]{4,3,0,1,2:T(8,128)(2,1)} async-done(((bf16[8,1,64,8,512]{4,3,0,1,2:T(8,128)(2,1)}), bf16[8,1,64,8,512]{4,3,0,1,2:T(8,128)(2,1)}, u32[]{:S(2)}, u32[]{:S(2)}) %all-to-all-start.1) | async-done | bytes 4194336 | tf_op jit(solution)/shard_map/all_to_all | solution.py:79
  262.2 4.3 multiply_reduce_fusion.2
  266.5 0.9 multiply_reduce_fusion.3
  267.4 0.6 compare_select_fusion
  268.0 4.3 multiply_reduce_fusion
  272.3 12.4 %all-reduce.1 = (f32[64]{0:T(128)S(1)}, f32[8]{0:T(128)S(1)}, f32[8]{0:T(128)S(1)}) all-reduce(f32[64]{0:T(128)S(1)} %compare_select_fusion, f32[8]{0:T(128)S(1)} %get-tuple-element.3, f32[8]{0:T(128)S(1)} %get-tuple-element.2), channel_id=1, replica_groups=mesh['domain'=8,'fsdp'=64] {'domain'}, use_global_device_ids=true, to_apply=%region_5.6 | all-reduce | flops 80 | bytes 640 | tf_op jit(solution)/shard_map/psum | solution.py:55
  284.7 121.4 %all-reduce = (f32[64]{0:T(128)S(1)}, f32[8]{0:T(128)S(1)}, f32[8]{0:T(128)S(1)}) all-reduce(f32[64]{0:T(128)S(1)} %get-tuple-element.7, f32[8]{0:T(128)S(1)} %get-tuple-element.8, f32[8]{0:T(128)S(1)} %get-tuple-element.9), channel_id=1, replica_groups=mesh['domain'=8,'fsdp'=64] {'fsdp'}, use_global_device_ids=true, to_apply=%region_6.7 | all-reduce | flops 80 | bytes 640 | tf_op jit(solution)/shard_map/psum | solution.py:55
  406.1 0.6 dynamic_slice.9
  407.5 0.5 fusion.17
  408.0 1.9 collective-permute-start
  409.9 25.2 %collective-permute-done = f32[512,512]{1,0:T(8,128)S(1)} collective-permute-done((f32[512,512]{1,0:T(8,128)S(1)}, f32[512,512]{1,0:T(8,128)S(1)}, u32[]{:S(2)}, u32[]{:S(2)}) %collective-permute-start) | collective-permute-done | bytes 1048608 | tf_op jit(solution)/shard_map/ppermute | solution.py:17
  435.3 31.1 %collective-permute-start.1 = (f32[512,512]{1,0:T(8,128)S(1)}, f32[512,512]{1,0:T(8,128)S(1)}, u32[]{:S(2)}, u32[]{:S(2)}) collective-permute-start(f32[512,512]{1,0:T(8,128)S(1)} %add.119), channel_id=1, source_target_pairs={{0,2},{1,3},{2,0},{3,1},{4,6},{5,7},{6,4},{7,5},{8,10},{9,11},{10,... | collective-permute-start | bytes 3145736 | tf_op jit(solution)/shard_map/ppermute | solution.py:17
  466.4 31.7 %collective-permute-done.1 = f32[512,512]{1,0:T(8,128)S(1)} collective-permute-done((f32[512,512]{1,0:T(8,128)S(1)}, f32[512,512]{1,0:T(8,128)S(1)}, u32[]{:S(2)}, u32[]{:S(2)}) %collective-permute-start.1) | collective-permute-done | bytes 1048608 | tf_op jit(solution)/shard_map/ppermute | solution.py:17
  498.3 1.9 collective-permute-start.2
  500.2 51.2 %collective-permute-done.2 = f32[512,512]{1,0:T(8,128)S(1)} collective-permute-done((f32[512,512]{1,0:T(8,128)S(1)}, f32[512,512]{1,0:T(8,128)S(1)}, u32[]{:S(2)}, u32[]{:S(2)}) %collective-permute-start.2) | collective-permute-done | bytes 1048608 | tf_op jit(solution)/shard_map/ppermute | solution.py:17
  551.5 0.3 add_convert_fusion.5
  551.7 0.8 fusion
  552.5 0.5 fusion.18
  553.0 1.9 collective-permute-start.3
  554.9 21.2 %collective-permute-done.3 = f32[512,512]{1,0:T(8,128)S(1)} collective-permute-done((f32[512,512]{1,0:T(8,128)S(1)}, f32[512,512]{1,0:T(8,128)S(1)}, u32[]{:S(2)}, u32[]{:S(2)}) %collective-permute-start.3) | collective-permute-done | bytes 1048608 | tf_op jit(solution)/shard_map/ppermute | solution.py:17
  576.3 26.6 %collective-permute-start.4 = (f32[512,512]{1,0:T(8,128)S(1)}, f32[512,512]{1,0:T(8,128)S(1)}, u32[]{:S(2)}, u32[]{:S(2)}) collective-permute-start(f32[512,512]{1,0:T(8,128)S(1)} %add.124), channel_id=1, source_target_pairs={{0,2},{1,3},{2,0},{3,1},{4,6},{5,7},{6,4},{7,5},{8,10},{9,11},{10,... | collective-permute-start | bytes 3145736 | tf_op jit(solution)/shard_map/ppermute | solution.py:17
  602.9 23.8 %collective-permute-done.4 = f32[512,512]{1,0:T(8,128)S(1)} collective-permute-done((f32[512,512]{1,0:T(8,128)S(1)}, f32[512,512]{1,0:T(8,128)S(1)}, u32[]{:S(2)}, u32[]{:S(2)}) %collective-permute-start.4) | collective-permute-done | bytes 1048608 | tf_op jit(solution)/shard_map/ppermute | solution.py:17
  626.9 3.7 collective-permute-start.5
  630.6 84.6 %collective-permute-done.5 = f32[512,512]{1,0:T(8,128)S(1)} collective-permute-done((f32[512,512]{1,0:T(8,128)S(1)}, f32[512,512]{1,0:T(8,128)S(1)}, u32[]{:S(2)}, u32[]{:S(2)}) %collective-permute-start.5) | collective-permute-done | bytes 1048608 | tf_op jit(solution)/shard_map/ppermute | solution.py:17
  715.2 0.3 add_convert_fusion.3
  715.5 0.8 fusion.1
  716.3 0.5 fusion.19
  716.7 1.9 collective-permute-start.6
  718.6 18.2 %collective-permute-done.6 = f32[512,512]{1,0:T(8,128)S(1)} collective-permute-done((f32[512,512]{1,0:T(8,128)S(1)}, f32[512,512]{1,0:T(8,128)S(1)}, u32[]{:S(2)}, u32[]{:S(2)}) %collective-permute-start.6) | collective-permute-done | bytes 1048608 | tf_op jit(solution)/shard_map/ppermute | solution.py:17
  737.1 1.9 collective-permute-start.7
  739.0 37.0 %collective-permute-done.7 = f32[512,512]{1,0:T(8,128)S(1)} collective-permute-done((f32[512,512]{1,0:T(8,128)S(1)}, f32[512,512]{1,0:T(8,128)S(1)}, u32[]{:S(2)}, u32[]{:S(2)}) %collective-permute-start.7) | collective-permute-done | bytes 1048608 | tf_op jit(solution)/shard_map/ppermute | solution.py:17
  776.2 3.3 collective-permute-start.8
  779.5 47.3 %collective-permute-done.8 = f32[512,512]{1,0:T(8,128)S(1)} collective-permute-done((f32[512,512]{1,0:T(8,128)S(1)}, f32[512,512]{1,0:T(8,128)S(1)}, u32[]{:S(2)}, u32[]{:S(2)}) %collective-permute-start.8) | collective-permute-done | bytes 1048608 | tf_op jit(solution)/shard_map/ppermute | solution.py:17
  826.8 0.3 add_convert_fusion.1
  827.0 1.6 fusion.2
  828.6 27.0 %all-to-all-start.2 = ((bf16[1,64,8,512]{3,2,0,1:T(8,128)(2,1)}), bf16[1,64,8,512]{3,2,0,1:T(8,128)(2,1)S(1)}, u32[]{:S(2)}, u32[]{:S(2)}) async-start(bf16[1,64,8,512]{3,2,0,1:T(8,128)(2,1)} %bitcast.6), calls=%async_computation.2 | async-start | bytes 1048576 | tf_op jit(solution)/shard_map/all_to_all | solution.py:105
  855.6 0.7 reduce_sum.97
  857.1 1.3 fusion.16
  858.5 1.2 broadcast_divide_fusion
  859.7 17.6 %all-to-all-done.2 = bf16[1,64,8,512]{3,2,0,1:T(8,128)(2,1)S(1)} async-done(((bf16[1,64,8,512]{3,2,0,1:T(8,128)(2,1)}), bf16[1,64,8,512]{3,2,0,1:T(8,128)(2,1)S(1)}, u32[]{:S(2)}, u32[]{:S(2)}) %all-to-all-start.2) | async-done | bytes 524320 | tf_op jit(solution)/shard_map/all_to_all | solution.py:105
  877.3 1.1 convert_multiply_fusion
  (18 shorter events, 1.7 us)
Async XLA Ops:
  57.9 19.1 %copy-start = (f32[8]{0:T(128)S(1)}, f32[8]{0:T(128)}, u32[]{:S(2)}) copy-start(f32[8]{0:T(128)} %param.7) | copy-start | bytes 100
  57.9 19.7 %copy-start.1 = (s32[64]{0:T(128)S(1)}, s32[64]{0:T(128)}, u32[]{:S(2)}) copy-start(s32[64]{0:T(128)} %param.5) | copy-start | bytes 772
  57.9 20.3 %copy-start.2 = (s32[8]{0:T(128)S(1)}, s32[8]{0:T(128)}, u32[]{:S(2)}) copy-start(s32[8]{0:T(128)} %param.6) | copy-start | bytes 100
  57.9 204.3 %all-to-all-start.1 = ((bf16[8,1,64,8,512]{4,3,0,1,2:T(8,128)(2,1)}), bf16[8,1,64,8,512]{4,3,0,1,2:T(8,128)(2,1)}, u32[]{:S(2)}, u32[]{:S(2)}) async-start(bf16[8,1,64,8,512]{4,3,0,1,2:T(8,128)(2,1)} %copy.8), calls=%async_computation.1 | async-start | bytes 8388608 | tf_op jit(solution)/shard_map/all_to_all | solution.py:79
  408.0 27.1 %collective-permute-start = (f32[512,512]{1,0:T(8,128)S(1)}, f32[512,512]{1,0:T(8,128)S(1)}, u32[]{:S(2)}, u32[]{:S(2)}) collective-permute-start(f32[512,512]{1,0:T(8,128)S(1)} %fusion.17), channel_id=1, source_target_pairs={{0,1},{1,0},{2,3},{3,2},{4,5},{5,4},{6,7},{7,6},{8,9},{9,8},{10,11... | collective-permute-start | bytes 3145736 | tf_op jit(solution)/shard_map/ppermute | solution.py:17
  435.3 62.8 %collective-permute-start.1 = (f32[512,512]{1,0:T(8,128)S(1)}, f32[512,512]{1,0:T(8,128)S(1)}, u32[]{:S(2)}, u32[]{:S(2)}) collective-permute-start(f32[512,512]{1,0:T(8,128)S(1)} %add.119), channel_id=1, source_target_pairs={{0,2},{1,3},{2,0},{3,1},{4,6},{5,7},{6,4},{7,5},{8,10},{9,11},{10,... | collective-permute-start | bytes 3145736 | tf_op jit(solution)/shard_map/ppermute | solution.py:17
  498.3 53.2 %collective-permute-start.2 = (f32[512,512]{1,0:T(8,128)S(1)}, f32[512,512]{1,0:T(8,128)S(1)}, u32[]{:S(2)}, u32[]{:S(2)}) collective-permute-start(f32[512,512]{1,0:T(8,128)S(1)} %add.120), channel_id=1, source_target_pairs={{0,4},{1,5},{2,6},{3,7},{4,0},{5,1},{6,2},{7,3},{8,12},{9,13},{10,... | collective-permute-start | bytes 3145736 | tf_op jit(solution)/shard_map/ppermute | solution.py:17
  553.0 23.1 %collective-permute-start.3 = (f32[512,512]{1,0:T(8,128)S(1)}, f32[512,512]{1,0:T(8,128)S(1)}, u32[]{:S(2)}, u32[]{:S(2)}) collective-permute-start(f32[512,512]{1,0:T(8,128)S(1)} %fusion.18), channel_id=1, source_target_pairs={{0,1},{1,0},{2,3},{3,2},{4,5},{5,4},{6,7},{7,6},{8,9},{9,8},{10,11... | collective-permute-start | bytes 3145736 | tf_op jit(solution)/shard_map/ppermute | solution.py:17
  576.3 50.4 %collective-permute-start.4 = (f32[512,512]{1,0:T(8,128)S(1)}, f32[512,512]{1,0:T(8,128)S(1)}, u32[]{:S(2)}, u32[]{:S(2)}) collective-permute-start(f32[512,512]{1,0:T(8,128)S(1)} %add.124), channel_id=1, source_target_pairs={{0,2},{1,3},{2,0},{3,1},{4,6},{5,7},{6,4},{7,5},{8,10},{9,11},{10,... | collective-permute-start | bytes 3145736 | tf_op jit(solution)/shard_map/ppermute | solution.py:17
  626.9 88.3 %collective-permute-start.5 = (f32[512,512]{1,0:T(8,128)S(1)}, f32[512,512]{1,0:T(8,128)S(1)}, u32[]{:S(2)}, u32[]{:S(2)}) collective-permute-start(f32[512,512]{1,0:T(8,128)S(1)} %add.125), channel_id=1, source_target_pairs={{0,4},{1,5},{2,6},{3,7},{4,0},{5,1},{6,2},{7,3},{8,12},{9,13},{10,... | collective-permute-start | bytes 3145736 | tf_op jit(solution)/shard_map/ppermute | solution.py:17
  716.7 20.1 %collective-permute-start.6 = (f32[512,512]{1,0:T(8,128)S(1)}, f32[512,512]{1,0:T(8,128)S(1)}, u32[]{:S(2)}, u32[]{:S(2)}) collective-permute-start(f32[512,512]{1,0:T(8,128)S(1)} %fusion.19), channel_id=1, source_target_pairs={{0,1},{1,0},{2,3},{3,2},{4,5},{5,4},{6,7},{7,6},{8,9},{9,8},{10,11... | collective-permute-start | bytes 3145736 | tf_op jit(solution)/shard_map/ppermute | solution.py:17
  737.1 39.0 %collective-permute-start.7 = (f32[512,512]{1,0:T(8,128)S(1)}, f32[512,512]{1,0:T(8,128)S(1)}, u32[]{:S(2)}, u32[]{:S(2)}) collective-permute-start(f32[512,512]{1,0:T(8,128)S(1)} %add.129), channel_id=1, source_target_pairs={{0,2},{1,3},{2,0},{3,1},{4,6},{5,7},{6,4},{7,5},{8,10},{9,11},{10,... | collective-permute-start | bytes 3145736 | tf_op jit(solution)/shard_map/ppermute | solution.py:17
  776.2 50.6 %collective-permute-start.8 = (f32[512,512]{1,0:T(8,128)S(1)}, f32[512,512]{1,0:T(8,128)S(1)}, u32[]{:S(2)}, u32[]{:S(2)}) collective-permute-start(f32[512,512]{1,0:T(8,128)S(1)} %add.130), channel_id=1, source_target_pairs={{0,4},{1,5},{2,6},{3,7},{4,0},{5,1},{6,2},{7,3},{8,12},{9,13},{10,... | collective-permute-start | bytes 3145736 | tf_op jit(solution)/shard_map/ppermute | solution.py:17
  828.6 48.7 %all-to-all-start.2 = ((bf16[1,64,8,512]{3,2,0,1:T(8,128)(2,1)}), bf16[1,64,8,512]{3,2,0,1:T(8,128)(2,1)S(1)}, u32[]{:S(2)}, u32[]{:S(2)}) async-start(bf16[1,64,8,512]{3,2,0,1:T(8,128)(2,1)} %bitcast.6), calls=%async_computation.2 | async-start | bytes 1048576 | tf_op jit(solution)/shard_map/all_to_all | solution.py:105
